TPU v7x, 32 devices: a whole 2x2x4 slice. The times are simulated.
32 devices in a mesh: cell: 8 (over z, y), stn: 4 (over x, core).
Axes of the slice: x: 2, y: 2, z: 4, core: 2. Of those that a mesh axis runs over, the one named last changes fastest.
Arguments:
- cell_points: float32 [3, 8192], P(None, 'cell'), may hold values from 0 to 1
- magnetization: float32 [3, 8192], P(None, 'cell'), may hold values from -6 to 6
- cell_level: int32 [8192], P('cell'), may hold values from 0 to 2
- suscept: float32 [8192], P('cell'), may hold values from 0.2 to 2
- inducing: float32 [3], replicated, may hold values from -4 to 4
- stations: float32 [3, 4096], P(None, 'stn'), may hold values from 0 to 2, as said below
Outputs:
- updated: float32 [3, 8192], P(None, ('cell', 'stn'))
- predictions: float32 [4096], P(('stn', 'cell'))
Inputs may be any that keep to these rules, and one draw needn't show every extreme that they name: `stations`: the first two coordinates lie in the unit square; the third is 1 plus 0.5 to 2 times 8192 ** (-1/3).
All inputs are finite; a program needn't handle non-finite values.
Results may differ from a plain program's by a relative error of at most 0.0003.
Values sent between devices are 32-bit elements; how exact they have to be, the bound alone decides.
A program may use at most 64 MiB of HBM per device.

v0:
```python
import math

import jax
import jax.numpy as jnp
from jax import lax
from jax.sharding import PartitionSpec as P

INV_FOUR_PI = 0.25 / math.pi


def block_width(targets, sources):
    ceiling = max(256, (1 << 20) // targets)
    ceiling = 1 << ceiling.bit_length() - 1
    return math.gcd(sources, ceiling)


def pair_field(points, source_piece):
    delta_x = points[0][:, None] - source_piece[0][None, :]
    delta_y = points[1][:, None] - source_piece[1][None, :]
    delta_z = points[2][:, None] - source_piece[2][None, :]
    soften = source_piece[6][None, :]
    radius_sq = delta_x * delta_x + delta_y * delta_y + delta_z * delta_z + soften * soften
    inverse = lax.rsqrt(radius_sq)
    inverse_sq = inverse * inverse
    weight = INV_FOUR_PI * soften * soften * soften * inverse_sq * inverse
    projection = (
        3.0
        * (
            delta_x * source_piece[3][None, :]
            + delta_y * source_piece[4][None, :]
            + delta_z * source_piece[5][None, :]
        )
        * inverse_sq
    )
    field_x = jnp.sum(weight * (projection * delta_x - source_piece[3][None, :]), axis=1)
    field_y = jnp.sum(weight * (projection * delta_y - source_piece[4][None, :]), axis=1)
    field_z = jnp.sum(weight * (projection * delta_z - source_piece[5][None, :]), axis=1)
    return jnp.stack([field_x, field_y, field_z], 0)


def source_field(points, sources):
    number = sources.shape[1]
    blockw = block_width(points.shape[1], number)
    groups = sources.reshape(7, number // blockw, blockw).transpose(1, 0, 2)

    def advance(summed, source_piece):
        return (summed + pair_field(points, source_piece), None)

    result, unused = lax.scan(advance, jnp.zeros((3, points.shape[1]), jnp.float32), groups)
    return result


def shards(cell_points, magnetization, cell_level, suscept, inducing, stations):
    cycle_size = lax.axis_size("cell")
    section = lax.axis_size("stn")
    block_cells = cell_points.shape[1]
    spacing = float(block_cells * cycle_size * section // section) ** (-1.0 / 3.0)
    size_h = spacing * jnp.power(0.5, cell_level.astype(jnp.float32))
    packed = jnp.concatenate([cell_points, magnetization, size_h[None, :]], 0)
    owned = block_cells // section
    offset = lax.axis_index("stn") * owned
    targets = lax.dynamic_slice_in_dim(cell_points, offset, owned, 1)
    demag = source_field(targets, lax.all_gather(packed, "cell", axis=1, tiled=True))
    own_suscept = lax.dynamic_slice_in_dim(suscept, offset, owned, 0)
    updated = own_suscept[None, :] * (inducing[:, None] + demag)
    block_mag = lax.all_gather(updated, "stn", axis=1, tiled=True)
    moved = jnp.concatenate([cell_points, block_mag, size_h[None, :]], 0)
    field = source_field(stations, moved)
    predictions = lax.psum_scatter(
        jnp.sum(inducing[:, None] * field, axis=0), "cell", scatter_dimension=0, tiled=True
    )
    return (updated, predictions)


def solution(mesh):
    placed = (P(None, "cell"), P(None, "cell"), P("cell"), P("cell"), P(), P(None, "stn"))
    return jax.shard_map(
        shards,
        mesh=mesh,
        in_specs=placed,
        out_specs=(P(None, ("cell", "stn")), P(("stn", "cell"))),
        check_vma=False,
    )
```

profile of v0, /device:TPU:0, one launch (start us, length us, event | category | flops | bytes accessed | tf_op | source)
XLA Modules:
  0.0 82.9 jit_solution(14544340827631167878)
XLA Ops:
  0.6 0.7 constant_dynamic-slice_fusion.7
  1.3 0.7 multiply_multiply_fusion.3
  2.0 0.8 pad_maximum_fusion
  2.8 32.5 %all_gather.6 = f32[7,8192]{1,0:T(8,128)S(1)} all-gather(f32[7,1024]{1,0:T(8,128)S(1)} %pad_maximum_fusion), channel_id=1, replica_groups=mesh['cell'=8,'stn'=4] {'cell'}, dimensions={1}, use_global_device_ids=true | all-gather | bytes 258048 | tf_op jit(solution)/shard_map/all_gather | solution.py:63
  35.3 0.0 copy-start.3
  35.3 0.0 copy-start.2
  35.3 0.0 copy-start
  35.3 11.8 %while.3 = (s32[]{:T(128)}, f32[3,256]{1,0:T(4,128)S(1)}, f32[2,7,4096]{2,1,0:T(8,128)S(1)}, f32[3,256]{1,0:T(4,128)S(1)}, s32[]{:T(128)}, /*index=5*/s32[]{:T(128)}, s32[]{}, s32[]{}, s32[]{}, s32[]{}, /*index=10*/s32[]{}, s32[]{}) while((s32[]{:T(128)}, f32[3,256]{1,0:T(4,128)S(1)}, f32[2,7,4096]{2,1,0:T(8,128)S(1)}, ...), condition=%wide.region_4.5_spmd.clone, body=%wide.region_0.4_spmd.clone.sunk | while | flops 32524552 | bytes 431331 | solution.py:49
  35.3 0.1 constant_dynamic-slice_fusion.9
  35.5 5.7 %fusion.44 = (f32[256]{0:T(256)S(1)}, f32[256]{0:T(256)S(1)}, f32[256]{0:T(256)S(1)}) fusion(f32[4096]{0:T(1024)S(1)} %bitcast.60, f32[4096]{0:T(1024)S(1)} %bitcast.62, f32[256]{0:T(256)S(1)} %bitcast.69, f32[4096]{0:T(1024)S(1)} %get-tuple-element.134, f32[4096]{0:T(1024)S(1)} %bitcast.63, f32[4096]{0:T(1024)S(1)} %bitcast.61, f32[256]{0:T(256)S(1)} %bitcast.68, ...), kind=kLoop, calls=%fused_computation.19.clone.1 | loop fusion | flops 32505088 | bytes 137216 | tf_op jit(solution)/shard_map/while/body/eval_jaxpr/reduce_sum | solution.py:35
  41.2 0.1 constant_dynamic-slice_fusion.9
  41.4 5.7 %fusion.44 = (f32[256]{0:T(256)S(1)}, f32[256]{0:T(256)S(1)}, f32[256]{0:T(256)S(1)}) fusion(f32[4096]{0:T(1024)S(1)} %bitcast.60, f32[4096]{0:T(1024)S(1)} %bitcast.62, f32[256]{0:T(256)S(1)} %bitcast.69, f32[4096]{0:T(1024)S(1)} %get-tuple-element.134, f32[4096]{0:T(1024)S(1)} %bitcast.63, f32[4096]{0:T(1024)S(1)} %bitcast.61, f32[256]{0:T(256)S(1)} %bitcast.68, ...), kind=kLoop, calls=%fused_computation.19.clone.1 | loop fusion | flops 32505088 | bytes 137216 | tf_op jit(solution)/shard_map/while/body/eval_jaxpr/reduce_sum | solution.py:35
  47.2 0.8 dynamic_slice.13
  47.9 0.0 copy-done.3
  47.9 0.1 add_multiply_fusion
  48.0 0.0 copy-start.1
  48.0 5.2 %all_gather.7 = f32[3,1024]{1,0:T(4,128)S(1)} all-gather(f32[3,256]{1,0:T(4,128)S(1)} %add_multiply_fusion), channel_id=1, replica_groups=mesh['cell'=8,'stn'=4] {'stn'}, dimensions={1}, use_global_device_ids=true | all-gather | bytes 15360 | tf_op jit(solution)/shard_map/all_gather | solution.py:66
  53.2 0.0 copy-done.2
  53.2 0.0 copy-done
  53.2 0.0 copy-start.4
  53.3 6.2 %fusion.27 = (f32[1024]{0:T(1024)S(1)}, f32[1024]{0:T(1024)S(1)}, f32[1024]{0:T(1024)S(1)}) fusion(f32[1024]{0:T(1024)S(1)} %bitcast.73, f32[1024]{0:T(1024)S(1)} %bitcast.78, f32[1024]{0:T(1024)S(1)} %bitcast.75, f32[1024]{0:T(1024)S(1)} %get-tuple-element.88, f32[1024]{0:T(1024)S(1)} %bitcast.72, f32[1024]{0:T(1024)S(1)} %bitcast.79, ...), kind=kLoop, calls=%fused_computation.55 | loop fusion | flops 32502784 | bytes 57344 | tf_op jit(solution)/shard_map/while/body/eval_jaxpr/reduce_sum | solution.py:35
  59.5 0.0 copy-done.1
  59.5 0.1 fusion.34
  59.6 21.4 %all-reduce = f32[1024]{0:T(1024)S(1)} all-reduce(f32[1024]{0:T(1024)S(1)} %fusion.34), channel_id=2, replica_groups=mesh['cell'=8,'stn'=4] {'cell'}, use_global_device_ids=true, to_apply=%region_9.10.clone | all-reduce | flops 1024 | bytes 8192
  81.0 0.0 copy-done.4
  81.0 0.6 dynamic-slice.1
  82.3 0.6 dynamic-slice.2
  (10 shorter events, 0.1 us)
Async XLA Ops:
  35.3 12.6 %copy-start.3 = (f32[3]{0:T(128)S(1)}, f32[3]{0:T(128)}, u32[]{:S(2)}) copy-start(f32[3]{0:T(128)} %param.12) | copy-start | bytes 40
  35.3 17.9 %copy-start.2 = (f32[3,1024]{1,0:T(4,128)S(1)}, f32[3,1024]{1,0:T(4,128)}, u32[]{:S(2)}) copy-start(f32[3,1024]{1,0:T(4,128)} %param.13) | copy-start | bytes 36868
  35.3 17.9 %copy-start = (f32[3,1024]{1,0:T(4,128)S(1)}, f32[3,1024]{1,0:T(4,128)}, u32[]{:S(2)}) copy-start(f32[3,1024]{1,0:T(4,128)} %param.8) | copy-start | bytes 36868
  48.0 11.5 %copy-start.1 = (f32[3,256]{1,0:T(4,128)}, f32[3,256]{1,0:T(4,128)S(1)}, u32[]{:S(2)}) copy-start(f32[3,256]{1,0:T(4,128)S(1)} %add_multiply_fusion) | copy-start | bytes 9220
  53.2 27.8 %copy-start.4 = (u32[32]{0:T(128)S(1)}, u32[32]{0:T(128)}, u32[]{:S(2)}) copy-start(u32[32]{0:T(128)} %constant.48) | copy-start | bytes 388
where the time goes:
time: 83.3 us; the launch traced here: 82.9 us
  blocking collectives  59.1 us (71%)
  other arithmetic  19.4 us (23%)
  local copies, waits for them, and re-layouts  2.93 us (4%)
  between operations  1.37 us (2%)
    all_gather x1, blocking collectives, shards(): lax.all_gather(packed, 'cell', axis=1, tiled=True)  32.5 us
    unnamed x1, blocking collectives  21.4 us
    reduce_sum x3, other arithmetic, pair_field(): jnp.sum(weight * (projection * delta_x - source_piece[3][None, :]), axis=1)  17.7 us
    all_gather x1, blocking collectives, shards(): block_mag = lax.all_gather(updated, 'stn', axis=1, tiled=True)  5.17 us

commit v1 on v0

v1 whole, which is shorter than its diff:
```python
import functools
import math

import jax
import jax.numpy as jnp
from jax import lax
from jax.experimental import pallas as pl
from jax.experimental.pallas import tpu as pltpu
from jax.sharding import PartitionSpec as P

INV_FOUR_PI = 0.25 / math.pi
MESH = pl.DeviceIdType.MESH
LANES = 128
ROWS = 32


def partner(me, k, n):
    out, bit = 0, 1
    while bit < n:
        out = out + bit * (((me // bit) % 2 + (k // bit) % 2) % 2)
        bit *= 2
    return out


def lane_sums(values):
    ones = jnp.ones((8, LANES), jnp.float32)
    return lax.dot_general(
        ones,
        values,
        (((1,), (1,)), ((), ())),
        precision=lax.Precision.HIGHEST,
        preferred_element_type=jnp.float32,
    )


def kernel(
    nc, ns, cp, mg, lv, su, ind, st, upd, pred,
    pack, gath, tgt, acc, xi, mag, stb, racc, pbuf, rbuf,
    send1, recv1, send2, recv2, send3, recv3,
):
    block = cp.shape[1]
    owned = block // ns
    stations = st.shape[1]
    spacing = float(block * nc) ** (-1.0 / 3.0)
    c_me = lax.axis_index("cell")
    s_me = lax.axis_index("stn")

    barrier = pltpu.get_barrier_semaphore()

    @pl.loop(1, nc)
    def _(k):
        pl.semaphore_signal(barrier, inc=1, device_id={"cell": partner(c_me, k, nc)}, device_id_type=MESH)

    @pl.loop(1, ns)
    def _(k):
        pl.semaphore_signal(barrier, inc=1, device_id={"stn": partner(s_me, k, ns)}, device_id_type=MESH)

    level = lv[...]
    size_h = spacing * jnp.where(level == 0, 1.0, jnp.where(level == 1, 0.5, 0.25))
    strength = INV_FOUR_PI * size_h * size_h * size_h
    pack[0:3, :] = cp[...]
    pack[3:6, :] = mg[...] * strength
    pack[6:7, :] = size_h * size_h
    pack[7:8, :] = strength

    pl.semaphore_wait(barrier, nc - 1 + ns - 1)

    def copy1(k):
        return pltpu.make_async_remote_copy(
            src_ref=pack, dst_ref=gath.at[k - 1], send_sem=send1.at[k - 1], recv_sem=recv1.at[k - 1],
            device_id={"cell": partner(c_me, k, nc)}, device_id_type=MESH,
        )

    @pl.loop(1, nc)
    def _(k):
        copy1(k).start()

    offset = s_me * owned
    ix, iy, iz = ind[0], ind[1], ind[2]
    for d in range(3):
        for t in range(owned // LANES):
            row = cp[d : d + 1, pl.ds(pl.multiple_of(offset + t * LANES, LANES), LANES)]
            tgt[d, t * LANES : (t + 1) * LANES, :] = jnp.broadcast_to(row, (LANES, LANES)).T
    acc[...] = jnp.zeros_like(acc)

    def sweep(src):
        @pl.loop(0, owned // ROWS)
        def _(g):
            rows = pl.ds(pl.multiple_of(g * ROWS, ROWS), ROWS)
            px, py, pz = tgt[0, rows, :], tgt[1, rows, :], tgt[2, rows, :]

            def chunks(start, count, sums):
                ax, ay, az = sums
                for j in range(count):
                    at = pl.ds(start + j * LANES, LANES)

                    def row(r):
                        return jnp.broadcast_to(src[r : r + 1, at], (ROWS, LANES))

                    dx, dy, dz = px - row(0), py - row(1), pz - row(2)
                    mx, my, mz = row(3), row(4), row(5)
                    inv = lax.rsqrt(dx * dx + dy * dy + dz * dz + row(6))
                    inv2 = inv * inv
                    inv3 = inv2 * inv
                    along = 3.0 * (dx * mx + dy * my + dz * mz) * inv2
                    ax = ax + inv3 * (along * dx - mx)
                    ay = ay + inv3 * (along * dy - my)
                    az = az + inv3 * (along * dz - mz)
                return ax, ay, az

            sums = (acc[0, rows, :], acc[1, rows, :], acc[2, rows, :])
            step = 8
            total = block // (LANES * step)
            if total == 1:
                sums = chunks(0, step, sums)
            else:
                sums = lax.fori_loop(
                    0, total, lambda i, s: chunks(pl.multiple_of(i * step * LANES, LANES), step, s), sums
                )
            acc[0, rows, :], acc[1, rows, :], acc[2, rows, :] = sums

    sweep(pack)

    @pl.loop(0, stations // LANES)
    def _(t):
        at = pl.ds(pl.multiple_of(t * LANES, LANES), LANES)
        x, y, z = [jnp.broadcast_to(st[d : d + 1, at], (LANES, LANES)).T for d in range(3)]
        stb[0, at, :] = x
        stb[1, at, :] = y
        stb[2, at, :] = z
        stb[3, at, :] = x * ix + y * iy + z * iz

    xi[...] = cp[0:1, :] * ix + cp[1:2, :] * iy + cp[2:3, :] * iz
    racc[...] = jnp.zeros_like(racc)

    @pl.loop(1, nc)
    def _(k):
        copy1(k).wait_recv()
        sweep(gath.at[k - 1])

    own = pl.ds(pl.multiple_of(offset, LANES), owned)
    gain = su[0:1, own]
    c_own = pack[7:8, own]
    new = [gain * (i + lane_sums(acc[d])[0:1]) for d, i in enumerate((ix, iy, iz))]
    for d in range(3):
        mag[s_me, d : d + 1, :] = 3.0 * c_own * new[d]
    mag[s_me, 3:4, :] = c_own * (new[0] * ix + new[1] * iy + new[2] * iz)

    def copy2(k):
        return pltpu.make_async_remote_copy(
            src_ref=mag.at[s_me], dst_ref=mag.at[s_me], send_sem=send2.at[k - 1], recv_sem=recv2.at[k - 1],
            device_id={"stn": partner(s_me, k, ns)}, device_id_type=MESH,
        )

    @pl.loop(1, ns)
    def _(k):
        copy2(k).start()

    for d in range(3):
        upd[d : d + 1, :] = new[d]

    def predict(k):
        who = partner(s_me, k, ns)

        @pl.loop(0, stations // ROWS)
        def _(g):
            rows = pl.ds(pl.multiple_of(g * ROWS, ROWS), ROWS)
            px, py, pz, pi = stb[0, rows, :], stb[1, rows, :], stb[2, rows, :], stb[3, rows, :]
            total = racc[rows, :]
            for j in range(owned // LANES):
                at = pl.ds(pl.multiple_of(who * owned + j * LANES, LANES), LANES)
                here = slice(j * LANES, (j + 1) * LANES)

                def spread(row):
                    return jnp.broadcast_to(row, (ROWS, LANES))

                dx, dy, dz = [p - spread(pack[d : d + 1, at]) for d, p in enumerate((px, py, pz))]
                mx, my, mz = [spread(mag[who, d : d + 1, here]) for d in range(3)]
                inv = lax.rsqrt(dx * dx + dy * dy + dz * dz + spread(pack[6:7, at]))
                inv2 = inv * inv
                both = (dx * mx + dy * my + dz * mz) * (pi - spread(xi[0:1, at]))
                total = total + (both * inv2 - spread(mag[who, 3:4, here])) * (inv2 * inv)
            racc[rows, :] = total

    predict(0)

    @pl.loop(1, ns)
    def _(k):
        copy2(k).wait_recv()
        predict(k)

    summed = lane_sums(racc[...])
    for c in range(nc):
        pbuf[c] = summed[:, c * LANES : (c + 1) * LANES]

    def copy3(k):
        who = partner(c_me, k, nc)
        return pltpu.make_async_remote_copy(
            src_ref=pbuf.at[who], dst_ref=rbuf.at[k - 1], send_sem=send3.at[k - 1], recv_sem=recv3.at[k - 1],
            device_id={"cell": who}, device_id_type=MESH,
        )

    @pl.loop(1, nc)
    def _(k):
        copy3(k).start()

    @pl.loop(1, nc)
    def _(k):
        copy3(k).wait_recv()

    result = pbuf[c_me]
    for k in range(nc - 1):
        result = result + rbuf[k]
    pred[...] = result[0:1]

    @pl.loop(1, nc)
    def _(k):
        copy1(k).wait_send()
        copy3(k).wait_send()

    @pl.loop(1, ns)
    def _(k):
        copy2(k).wait_send()


def shards(cell_points, magnetization, cell_level, suscept, inducing, stations):
    nc = lax.axis_size("cell")
    ns = lax.axis_size("stn")
    block = cell_points.shape[1]
    owned = block // ns
    targets = stations.shape[1]
    share = targets // nc
    f32 = jnp.float32
    vmem = pl.BlockSpec(memory_space=pltpu.VMEM)
    smem = pl.BlockSpec(memory_space=pltpu.SMEM)
    dma = pltpu.SemaphoreType.DMA
    updated, predictions = pl.pallas_call(
        functools.partial(kernel, nc, ns),
        out_shape=(jax.ShapeDtypeStruct((3, owned), f32), jax.ShapeDtypeStruct((1, share), f32)),
        in_specs=[vmem, vmem, vmem, vmem, smem, vmem],
        out_specs=(vmem, vmem),
        scratch_shapes=[
            pltpu.VMEM((8, block), f32),
            pltpu.VMEM((nc - 1, 8, block), f32),
            pltpu.VMEM((3, owned, LANES), f32),
            pltpu.VMEM((3, owned, LANES), f32),
            pltpu.VMEM((1, block), f32),
            pltpu.VMEM((ns, 8, owned), f32),
            pltpu.VMEM((4, targets, LANES), f32),
            pltpu.VMEM((targets, LANES), f32),
            pltpu.VMEM((nc, 8, share), f32),
            pltpu.VMEM((nc - 1, 8, share), f32),
            dma((nc - 1,)),
            dma((nc - 1,)),
            dma((ns - 1,)),
            dma((ns - 1,)),
            dma((nc - 1,)),
            dma((nc - 1,)),
        ],
        compiler_params=pltpu.CompilerParams(
            collective_id=0, has_side_effects=True, vmem_limit_bytes=40 * 1024 * 1024
        ),
    )(
        cell_points,
        magnetization,
        cell_level.reshape(1, block),
        suscept.reshape(1, block),
        inducing,
        stations,
    )
    return updated, predictions.reshape(share)


def solution(mesh):
    placed = (P(None, "cell"), P(None, "cell"), P("cell"), P("cell"), P(), P(None, "stn"))
    return jax.shard_map(
        shards,
        mesh=mesh,
        in_specs=placed,
        out_specs=(P(None, ("cell", "stn")), P(("stn", "cell"))),
        check_vma=False,
    )
```

time: 83.3 us -> 34.1 us (0.41)
  blocking collectives: 59.1 us -> 0 us
  Pallas kernels: 0 us -> 27.7 us
  other arithmetic: 19.4 us -> 0 us
  local copies, waits for them, and re-layouts: 2.93 us -> 5.28 us
    all_gather x2 -> x0, blocking collectives: 37.7 us -> none  [the longest x1 32.5 us: shards(): lax.all_gather(packed, 'cell', axis=1, tiled=True)]
    pallas_call x0 -> x1, Pallas kernels: none -> 27.7 us  [shards(): pl.pallas_call(functools.partial(kernel, nc, ns), out_shape=(jax.ShapeDty...]
    unnamed x1 -> x0, blocking collectives: 21.4 us -> none
    reduce_sum x4 -> x0, other arithmetic: 17.8 us -> none  [the longest x3 17.7 us: pair_field(): jnp.sum(weight * (projection * delta_x - source_piece[3][None, :]), axis=1)]
    unnamed x12 -> x14, local copies, waits for them, and re-layouts: 1.19 us -> 5.28 us
    dynamic_slice x2 -> x0, local copies, waits for them, and re-layouts: 1.46 us -> none  [the longest x1 0.77 us: shards(): own_suscept = lax.dynamic_slice_in_dim(suscept, offset, owned, 0)]
where the time goes in v1:
time: 34.1 us; the launch traced here: 33.7 us
  Pallas kernels  27.7 us (81%)
  local copies, waits for them, and re-layouts  5.28 us (15%)
  between operations  0.65 us (2%)
    pallas_call x1, Pallas kernels, shards(): pl.pallas_call(functools.partial(kernel, nc, ns), out_shape=(jax.ShapeDty...  27.7 us
    unnamed x14, local copies, waits for them, and re-layouts  5.28 us

profile of v1, /device:TPU:0, one launch (start us, length us, event | category | flops | bytes accessed | tf_op | source)
XLA Modules:
  0.0 33.7 jit_solution(641374447179406292)
XLA Ops:
  0.6 0.0 copy-start.5
  0.6 0.6 %copy-done.5 = f32[3]{0:T(128)S(1)} copy-done((f32[3]{0:T(128)S(1)}, f32[3]{0:T(128)}, u32[]{:S(2)}) %copy-start.5) | copy-done | bytes 36
  1.3 0.0 copy-start
  1.3 0.7 %copy-done = f32[3,1024]{1,0:T(4,128)S(1)} copy-done((f32[3,1024]{1,0:T(4,128)S(1)}, f32[3,1024]{1,0:T(4,128)}, u32[]{:S(2)}) %copy-start) | copy-done | bytes 12312
  2.0 0.0 copy-start.1
  2.0 0.7 %copy-done.1 = f32[3,1024]{1,0:T(4,128)S(1)} copy-done((f32[3,1024]{1,0:T(4,128)S(1)}, f32[3,1024]{1,0:T(4,128)}, u32[]{:S(2)}) %copy-start.1) | copy-done | bytes 12312
  2.7 0.0 copy-start.2
  2.7 0.7 %copy-done.2 = f32[3,1024]{1,0:T(4,128)S(1)} copy-done((f32[3,1024]{1,0:T(4,128)S(1)}, f32[3,1024]{1,0:T(4,128)}, u32[]{:S(2)}) %copy-start.2) | copy-done | bytes 12312
  3.4 0.0 copy-start.3
  3.4 0.7 %copy-done.3 = s32[1024]{0:T(1024)S(1)} copy-done((s32[1024]{0:T(1024)S(1)}, s32[1024]{0:T(1024)}, u32[]{:S(2)}) %copy-start.3) | copy-done | bytes 4120
  4.1 0.0 copy-start.4
  4.1 0.7 %copy-done.4 = f32[1024]{0:T(1024)S(1)} copy-done((f32[1024]{0:T(1024)S(1)}, f32[1024]{0:T(1024)}, u32[]{:S(2)}) %copy-start.4) | copy-done | bytes 4120
  4.8 27.7 %shard_map.77 = (f32[3,256]{1,0:T(4,128)S(1)}, f32[1,128]{1,0:T(1,128)S(1)}) custom-call(f32[3,1024]{1,0:T(4,128)S(1)} %copy-done, f32[3,1024]{1,0:T(4,128)S(1)} %copy-done.1, s32[1,1024]{1,0:T(1,128)S(1)} %bitcast.3, f32[1,1024]{1,0:T(1,128)S(1)} %bitcast.4, f32[3]{0:T(128)S(1)} %copy-done.5, f32[3,1024]{1,0:T(4,128)S(1)} %copy-done.2), custom_call_target="tpu_custom_call" | custom-call | tf_op jit(solution)/shard_map/pallas_call | solution.py:237
  32.6 0.6 %copy.10 = f32[3,256]{1,0:T(4,128)} copy(f32[3,256]{1,0:T(4,128)S(1)} %get-tuple-element.8) | data formatting | bytes 6144
  33.2 0.5 %copy.11 = f32[128]{0:T(128)} copy(f32[128]{0:T(128)S(1)} %bitcast.5) | data formatting | bytes 1024
Async XLA Ops:
  0.6 0.7 %copy-start.5 = (f32[3]{0:T(128)S(1)}, f32[3]{0:T(128)}, u32[]{:S(2)}) copy-start(f32[3]{0:T(128)} %ind.1) | copy-start | bytes 40
  1.3 0.7 %copy-start = (f32[3,1024]{1,0:T(4,128)S(1)}, f32[3,1024]{1,0:T(4,128)}, u32[]{:S(2)}) copy-start(f32[3,1024]{1,0:T(4,128)} %cp.1) | copy-start | bytes 36868
  2.0 0.7 %copy-start.1 = (f32[3,1024]{1,0:T(4,128)S(1)}, f32[3,1024]{1,0:T(4,128)}, u32[]{:S(2)}) copy-start(f32[3,1024]{1,0:T(4,128)} %mg.1) | copy-start | bytes 36868
  2.7 0.7 %copy-start.2 = (f32[3,1024]{1,0:T(4,128)S(1)}, f32[3,1024]{1,0:T(4,128)}, u32[]{:S(2)}) copy-start(f32[3,1024]{1,0:T(4,128)} %st.1) | copy-start | bytes 36868
  3.4 0.7 %copy-start.3 = (s32[1024]{0:T(1024)S(1)}, s32[1024]{0:T(1024)}, u32[]{:S(2)}) copy-start(s32[1024]{0:T(1024)} %param.8) | copy-start | bytes 12292
  4.1 0.7 %copy-start.4 = (f32[1024]{0:T(1024)S(1)}, f32[1024]{0:T(1024)}, u32[]{:S(2)}) copy-start(f32[1024]{0:T(1024)} %param.9) | copy-start | bytes 12292

commit v2 on v1

v2 whole, which is shorter than its diff:
```python
import functools
import math

import jax
import jax.numpy as jnp
from jax import lax
from jax.experimental import pallas as pl
from jax.experimental.pallas import tpu as pltpu
from jax.sharding import PartitionSpec as P

INV_FOUR_PI = 0.25 / math.pi
MESH = pl.DeviceIdType.MESH
LANES = 128
ROWS = 32


def partner(me, k, n):
    out, bit = 0, 1
    while bit < n:
        out = out + bit * (((me // bit) % 2 + (k // bit) % 2) % 2)
        bit *= 2
    return out


def lane_sums(values):
    ones = jnp.ones((8, LANES), jnp.float32)
    return lax.dot_general(
        ones,
        values,
        (((1,), (1,)), ((), ())),
        precision=lax.Precision.HIGHEST,
        preferred_element_type=jnp.float32,
    )


def kernel(
    nc, ns, cp_hbm, mg_hbm, lv_hbm, su_hbm, ind_hbm, st_hbm, upd, pred,
    cp, mg, lv, su, ind, st, cvol, gath, tgt, acc, mag, stb, racc,
    send1, recv1, send2, recv2, loaded,
):
    loads = [
        pltpu.make_async_copy(src, dst, loaded.at[i])
        for i, (src, dst) in enumerate(
            ((lv_hbm, lv), (mg_hbm, mg), (cp_hbm, cp), (ind_hbm, ind), (st_hbm, st), (su_hbm, su))
        )
    ]
    for load in loads:
        load.start()
    block = cp.shape[1]
    owned = block // ns
    share = st.shape[1] // nc
    spacing = float(block * nc) ** (-1.0 / 3.0)
    c_me = lax.axis_index("cell")
    s_me = lax.axis_index("stn")

    barrier = pltpu.get_barrier_semaphore()

    @pl.loop(1, nc)
    def _(k):
        pl.semaphore_signal(barrier, inc=1, device_id={"cell": partner(c_me, k, nc)}, device_id_type=MESH)

    @pl.loop(1, ns)
    def _(k):
        pl.semaphore_signal(barrier, inc=1, device_id={"stn": partner(s_me, k, ns)}, device_id_type=MESH)

    for load in loads[:4]:
        load.wait()
    ix, iy, iz = ind[0], ind[1], ind[2]
    level = lv[...]
    size_h = spacing * jnp.where(level == 0, 1.0, jnp.where(level == 1, 0.5, 0.25))
    strength = INV_FOUR_PI * size_h * size_h * size_h
    pack = gath.at[0]
    pack[0:3, :] = cp[...]
    pack[3:6, :] = mg[...] * strength
    pack[6:7, :] = size_h * size_h
    pack[7:8, :] = cp[0:1, :] * ix + cp[1:2, :] * iy + cp[2:3, :] * iz
    cvol[...] = strength

    pl.semaphore_wait(barrier, nc - 1 + ns - 1)

    def copy1(k):
        return pltpu.make_async_remote_copy(
            src_ref=gath.at[0], dst_ref=gath.at[k], send_sem=send1.at[k], recv_sem=recv1.at[k],
            device_id={"cell": partner(c_me, k, nc)}, device_id_type=MESH,
        )

    @pl.loop(1, nc)
    def _(k):
        copy1(k).start()

    offset = s_me * owned
    own = pl.ds(pl.multiple_of(offset, LANES), owned)
    for d in range(3):
        for t in range(owned // LANES):
            row = cp[d : d + 1, pl.ds(pl.multiple_of(offset + t * LANES, LANES), LANES)]
            tgt[d, t * LANES : (t + 1) * LANES, :] = jnp.broadcast_to(row, (LANES, LANES)).T
    acc[...] = jnp.zeros_like(acc)

    for load in loads[4:]:
        load.wait()
    mine = pl.ds(pl.multiple_of(c_me * share, LANES), share)
    place = [jnp.broadcast_to(st[d : d + 1, mine], (LANES, share)).T for d in range(3)]
    for d in range(3):
        stb[d] = place[d]
    stb[3] = place[0] * ix + place[1] * iy + place[2] * iz
    racc[...] = jnp.zeros_like(racc)

    def sweep(src):
        @pl.loop(0, owned // ROWS)
        def _(g):
            rows = pl.ds(pl.multiple_of(g * ROWS, ROWS), ROWS)
            px, py, pz = tgt[0, rows, :], tgt[1, rows, :], tgt[2, rows, :]

            def chunks(start, count, sums):
                ax, ay, az = sums
                for j in range(count):
                    at = pl.ds(start + j * LANES, LANES)

                    def row(r):
                        return jnp.broadcast_to(src[r : r + 1, at], (ROWS, LANES))

                    dx, dy, dz = px - row(0), py - row(1), pz - row(2)
                    mx, my, mz = row(3), row(4), row(5)
                    inv = lax.rsqrt(dx * dx + dy * dy + dz * dz + row(6))
                    inv2 = inv * inv
                    inv3 = inv2 * inv
                    along = 3.0 * (dx * mx + dy * my + dz * mz) * inv2
                    ax = ax + inv3 * (along * dx - mx)
                    ay = ay + inv3 * (along * dy - my)
                    az = az + inv3 * (along * dz - mz)
                return ax, ay, az

            sums = (acc[0, rows, :], acc[1, rows, :], acc[2, rows, :])
            step = 8
            total = block // (LANES * step)
            if total == 1:
                sums = chunks(0, step, sums)
            else:
                sums = lax.fori_loop(
                    0, total, lambda i, s: chunks(pl.multiple_of(i * step * LANES, LANES), step, s), sums
                )
            acc[0, rows, :], acc[1, rows, :], acc[2, rows, :] = sums

    sweep(pack)

    @pl.loop(1, nc)
    def _(k):
        copy1(k).wait_recv()
        sweep(gath.at[k])

    gain = su[0:1, own]
    c_own = cvol[0:1, own]
    me = c_me * ns + s_me
    new = [gain * (i + lane_sums(acc[d])[0:1]) for d, i in enumerate((ix, iy, iz))]
    for d in range(3):
        mag[me, d : d + 1, :] = 3.0 * c_own * new[d]
    mag[me, 3:4, :] = c_own * (new[0] * ix + new[1] * iy + new[2] * iz)

    def copy2(k, slot):
        kc, ks = k // ns, k % ns
        return pltpu.make_async_remote_copy(
            src_ref=mag.at[me], dst_ref=mag.at[slot], send_sem=send2.at[k], recv_sem=recv2.at[slot],
            device_id={"cell": partner(c_me, kc, nc), "stn": partner(s_me, ks, ns)}, device_id_type=MESH,
        )

    @pl.loop(1, nc * ns)
    def _(k):
        copy2(k, me).start()

    for d in range(3):
        upd[d : d + 1, :] = new[d]

    def predict(kc, s_who, who):
        for j in range(owned // LANES):
            at = pl.ds(pl.multiple_of(s_who * owned + j * LANES, LANES), LANES)
            here = slice(j * LANES, (j + 1) * LANES)

            def spread(row):
                return jnp.broadcast_to(row, (share, LANES))

            dx, dy, dz = [stb[d] - spread(gath[kc, d : d + 1, at]) for d in range(3)]
            mx, my, mz = [spread(mag[who, d : d + 1, here]) for d in range(3)]
            inv = lax.rsqrt(dx * dx + dy * dy + dz * dz + spread(gath[kc, 6:7, at]))
            inv2 = inv * inv
            both = (dx * mx + dy * my + dz * mz) * (stb[3] - spread(gath[kc, 7:8, at]))
            racc[...] += (both * inv2 - spread(mag[who, 3:4, here])) * (inv2 * inv)

    predict(0, s_me, me)

    @pl.loop(1, nc * ns)
    def _(k):
        kc, ks = k // ns, k % ns
        s_who = partner(s_me, ks, ns)
        who = partner(c_me, kc, nc) * ns + s_who
        copy2(k, who).wait_recv()
        predict(kc, s_who, who)

    pred[...] = lane_sums(racc[...])[0:1]

    @pl.loop(1, nc)
    def _(k):
        copy1(k).wait_send()

    @pl.loop(1, nc * ns)
    def _(k):
        copy2(k, me).wait_send()


def shards(cell_points, magnetization, cell_level, suscept, inducing, stations):
    nc = lax.axis_size("cell")
    ns = lax.axis_size("stn")
    block = cell_points.shape[1]
    owned = block // ns
    targets = stations.shape[1]
    share = targets // nc
    f32 = jnp.float32
    vmem = pl.BlockSpec(memory_space=pltpu.VMEM)
    hbm = pl.BlockSpec(memory_space=pltpu.HBM)
    dma = pltpu.SemaphoreType.DMA
    updated, predictions = pl.pallas_call(
        functools.partial(kernel, nc, ns),
        out_shape=(jax.ShapeDtypeStruct((3, owned), f32), jax.ShapeDtypeStruct((1, share), f32)),
        in_specs=[hbm] * 6,
        out_specs=(vmem, vmem),
        scratch_shapes=[
            pltpu.VMEM((3, block), f32),
            pltpu.VMEM((3, block), f32),
            pltpu.VMEM((1, block), jnp.int32),
            pltpu.VMEM((1, block), f32),
            pltpu.SMEM((3,), f32),
            pltpu.VMEM((3, targets), f32),
            pltpu.VMEM((1, block), f32),
            pltpu.VMEM((nc, 8, block), f32),
            pltpu.VMEM((3, owned, LANES), f32),
            pltpu.VMEM((3, owned, LANES), f32),
            pltpu.VMEM((nc * ns, 4, owned), f32),
            pltpu.VMEM((4, share, LANES), f32),
            pltpu.VMEM((share, LANES), f32),
            dma((nc,)),
            dma((nc,)),
            dma((nc * ns,)),
            dma((nc * ns,)),
            dma((6,)),
        ],
        compiler_params=pltpu.CompilerParams(
            collective_id=0, has_side_effects=True, vmem_limit_bytes=60 * 1024 * 1024
        ),
    )(
        cell_points,
        magnetization,
        cell_level.reshape(1, block),
        suscept.reshape(1, block),
        inducing,
        stations,
    )
    return updated, predictions.reshape(share)


def solution(mesh):
    placed = (P(None, "cell"), P(None, "cell"), P("cell"), P("cell"), P(), P(None, "stn"))
    return jax.shard_map(
        shards,
        mesh=mesh,
        in_specs=placed,
        out_specs=(P(None, ("cell", "stn")), P(("stn", "cell"))),
        check_vma=False,
    )
```

time: 34.1 us -> 30.5 us (0.89)
  local copies, waits for them, and re-layouts: 5.28 us -> 1.82 us
    unnamed x14 -> x6, local copies, waits for them, and re-layouts: 5.28 us -> 1.82 us
where the time goes in v2:
time: 30.5 us; the launch traced here: 30.2 us
  Pallas kernels  27.8 us (91%)
  local copies, waits for them, and re-layouts  1.82 us (6%)
  between operations  0.65 us (2%)
    pallas_call x1, Pallas kernels, shards(): pl.pallas_call(functools.partial(kernel, nc, ns), out_shape=(jax.ShapeDty...  27.8 us
    unnamed x6, local copies, waits for them, and re-layouts  1.82 us

profile of v2, /device:TPU:0, one launch (start us, length us, event | category | flops | bytes accessed | tf_op | source)
XLA Modules:
  0.0 30.2 jit_solution(3476473720539733732)
XLA Ops:
  0.6 27.8 %shard_map.77 = (f32[3,256]{1,0:T(4,128)}, f32[1,128]{1,0:T(1,128)}) custom-call(f32[3,1024]{1,0:T(4,128)} %cp_hbm.1, f32[3,1024]{1,0:T(4,128)} %mg_hbm.1, s32[1,1024]{1,0:T(1,128)} %bitcast.3, f32[1,1024]{1,0:T(1,128)} %bitcast.4, f32[3]{0:T(128)} %ind_hbm.1, f32[3,1024]{1,0:T(4,128)} %st_hbm.1), custom_call_target="tpu_custom_call" | custom-call | tf_op jit(solution)/shard_map/pallas_call | solution.py:220
  28.4 0.0 copy-start
  28.4 0.7 %copy-done = f32[3,256]{1,0:T(4,128)S(1)} copy-done((f32[3,256]{1,0:T(4,128)S(1)}, f32[3,256]{1,0:T(4,128)}, u32[]{:S(2)}) %copy-start) | copy-done | bytes 3096
  29.1 0.0 copy-start.1
  29.1 0.6 %copy.10 = f32[3,256]{1,0:T(4,128)} copy(f32[3,256]{1,0:T(4,128)S(1)} %copy-done) | data formatting | bytes 6144
  29.7 0.0 copy-done.1
  29.7 0.5 %copy.11 = f32[128]{0:T(128)} copy(f32[128]{0:T(128)S(1)} %bitcast.5) | data formatting | bytes 1024
Async XLA Ops:
  28.4 0.7 %copy-start = (f32[3,256]{1,0:T(4,128)S(1)}, f32[3,256]{1,0:T(4,128)}, u32[]{:S(2)}) copy-start(f32[3,256]{1,0:T(4,128)} %get-tuple-element.8) | copy-start | bytes 9220
  29.1 0.6 %copy-start.1 = (f32[1,128]{1,0:T(1,128)S(1)}, f32[1,128]{1,0:T(1,128)}, u32[]{:S(2)}) copy-start(f32[1,128]{1,0:T(1,128)} %get-tuple-element.5) | copy-start | bytes 1540

commit v3 on v2

--- a/solution.py
+++ b/solution.py
@@ -35,7 +35,7 @@
 
 def kernel(
     nc, ns, cp_hbm, mg_hbm, lv_hbm, su_hbm, ind_hbm, st_hbm, upd, pred,
-    cp, mg, lv, su, ind, st, cvol, gath, tgt, acc, mag, stb, racc,
+    cp, mg, lv, su, ind, st, cvol, gath, tgt, acc, mag, stb, racc, geo, third,
     send1, recv1, send2, recv2, loaded,
 ):
     loads = [
@@ -106,6 +106,8 @@
     racc[...] = jnp.zeros_like(racc)
 
     def sweep(src):
+        third[...] = src[3:6, :] * (1.0 / 3.0)
+
         @pl.loop(0, owned // ROWS)
         def _(g):
             rows = pl.ds(pl.multiple_of(g * ROWS, ROWS), ROWS)
@@ -124,10 +126,13 @@
                     inv = lax.rsqrt(dx * dx + dy * dy + dz * dz + row(6))
                     inv2 = inv * inv
                     inv3 = inv2 * inv
-                    along = 3.0 * (dx * mx + dy * my + dz * mz) * inv2
-                    ax = ax + inv3 * (along * dx - mx)
-                    ay = ay + inv3 * (along * dy - my)
-                    az = az + inv3 * (along * dz - mz)
+                    along = (dx * mx + dy * my + dz * mz) * inv2
+                    tx, ty, tz = [
+                        jnp.broadcast_to(third[d : d + 1, at], (ROWS, LANES)) for d in range(3)
+                    ]
+                    ax = ax + inv3 * (along * dx - tx)
+                    ay = ay + inv3 * (along * dy - ty)
+                    az = az + inv3 * (along * dz - tz)
                 return ax, ay, az
 
             sums = (acc[0, rows, :], acc[1, rows, :], acc[2, rows, :])
@@ -151,59 +156,127 @@
     gain = su[0:1, own]
     c_own = cvol[0:1, own]
     me = c_me * ns + s_me
-    new = [gain * (i + lane_sums(acc[d])[0:1]) for d, i in enumerate((ix, iy, iz))]
+    new = [gain * (i + 3.0 * lane_sums(acc[d])[0:1]) for d, i in enumerate((ix, iy, iz))]
+    scaled = [3.0 * c_own * u for u in new]
     for d in range(3):
-        mag[me, d : d + 1, :] = 3.0 * c_own * new[d]
+        mag[me, d : d + 1, :] = scaled[d]
     mag[me, 3:4, :] = c_own * (new[0] * ix + new[1] * iy + new[2] * iz)
-
-    def copy2(k, slot):
-        kc, ks = k // ns, k % ns
+    here = [cp[d : d + 1, own] for d in range(3)]
+    mag[me, 4:5, :] = scaled[0] * here[0] + scaled[1] * here[1] + scaled[2] * here[2]
+
+    def copy2(c_who, s_who, slot, k):
         return pltpu.make_async_remote_copy(
             src_ref=mag.at[me], dst_ref=mag.at[slot], send_sem=send2.at[k], recv_sem=recv2.at[slot],
-            device_id={"cell": partner(c_me, kc, nc), "stn": partner(s_me, ks, ns)}, device_id_type=MESH,
+            device_id={"cell": c_who, "stn": s_who}, device_id_type=MESH,
         )
 
-    @pl.loop(1, nc * ns)
-    def _(k):
-        copy2(k, me).start()
+    s_others = [partner(s_me, ks, ns) for ks in range(ns)]
+    for ks in range(1, ns):
+        copy2(c_me, s_others[ks], me, ks).start()
+
+    @pl.loop(1, nc)
+    def _(kc):
+        c_who = partner(c_me, kc, nc)
+        for ks in range(ns):
+            copy2(c_who, s_others[ks], me, kc * ns + ks).start()
 
     for d in range(3):
         upd[d : d + 1, :] = new[d]
 
-    def predict(kc, s_who, who):
-        for j in range(owned // LANES):
-            at = pl.ds(pl.multiple_of(s_who * owned + j * LANES, LANES), LANES)
-            here = slice(j * LANES, (j + 1) * LANES)
-
-            def spread(row):
-                return jnp.broadcast_to(row, (share, LANES))
-
-            dx, dy, dz = [stb[d] - spread(gath[kc, d : d + 1, at]) for d in range(3)]
-            mx, my, mz = [spread(mag[who, d : d + 1, here]) for d in range(3)]
-            inv = lax.rsqrt(dx * dx + dy * dy + dz * dz + spread(gath[kc, 6:7, at]))
-            inv2 = inv * inv
-            both = (dx * mx + dy * my + dz * mz) * (stb[3] - spread(gath[kc, 7:8, at]))
-            racc[...] += (both * inv2 - spread(mag[who, 3:4, here])) * (inv2 * inv)
-
-    predict(0, s_me, me)
+    slots = geo.shape[0] // 2
+    chunks_in = block // LANES
+    part = min(8, chunks_in)
+
+    def spread(row):
+        return jnp.broadcast_to(row, (ROWS, LANES))
+
+    def over_pairs(body):
+        @pl.loop(0, share // ROWS)
+        def _(g):
+            rows = pl.ds(pl.multiple_of(g * ROWS, ROWS), ROWS)
+            for p in range(chunks_in // part):
+                body(rows, range(p * part, (p + 1) * part))
+
+    def geometry(kc, slot):
+        def body(rows, run):
+            px, py, pz, pi = stb[0, rows, :], stb[1, rows, :], stb[2, rows, :], stb[3, rows, :]
+            for j in run:
+                at = slice(j * LANES, (j + 1) * LANES)
+                dx, dy, dz = [p - spread(gath[kc, d : d + 1, at]) for d, p in enumerate((px, py, pz))]
+                inv = lax.rsqrt(dx * dx + dy * dy + dz * dz + spread(gath[kc, 6:7, at]))
+                inv2 = inv * inv
+                inv3 = inv2 * inv
+                geo[2 * slot, rows, at] = inv3
+                geo[2 * slot + 1, rows, at] = (pi - spread(gath[kc, 7:8, at])) * inv2 * inv3
+
+        over_pairs(body)
+
+    def predict(c_who, slot):
+        def body(rows, run):
+            px, py, pz = stb[0, rows, :], stb[1, rows, :], stb[2, rows, :]
+            total = racc[rows, :]
+            for j in run:
+                at = slice(j * LANES, (j + 1) * LANES)
+                start = j * LANES % owned
+                who = c_who * ns + j * LANES // owned
+
+                def row(r):
+                    return spread(mag[who, r : r + 1, start : start + LANES])
+
+                along = px * row(0) + py * row(1) + pz * row(2) - row(4)
+                total = total + (along * geo[2 * slot + 1, rows, at] - row(3) * geo[2 * slot, rows, at])
+            racc[rows, :] = total
+
+        over_pairs(body)
+
+    if slots > 1:
+
+        @pl.loop(0, nc)
+        def _(kc):
+            geometry(kc, kc)
+
+    for t in range(ns):
+
+        @pl.when(s_me != t)
+        def _():
+            slot = c_me * ns + t
+            copy2(c_me, t, slot, 0).wait_recv()
+
+    if slots == 1:
+        geometry(0, 0)
+    predict(c_me, 0)
+
+    @pl.loop(1, nc)
+    def _(kc):
+        c_who = partner(c_me, kc, nc)
+        for t in range(ns):
+            copy2(c_who, t, c_who * ns + t, 0).wait_recv()
+        if slots == 1:
+            geometry(kc, 0)
+            predict(c_who, 0)
+        else:
+            predict(c_who, kc)
+
+    pred[...] = lane_sums(racc[...])[0:1]
+
+    @pl.loop(1, nc)
+    def _(k):
+        copy1(k).wait_send()
 
     @pl.loop(1, nc * ns)
     def _(k):
-        kc, ks = k // ns, k % ns
-        s_who = partner(s_me, ks, ns)
-        who = partner(c_me, kc, nc) * ns + s_who
-        copy2(k, who).wait_recv()
-        predict(kc, s_who, who)
-
-    pred[...] = lane_sums(racc[...])[0:1]
-
-    @pl.loop(1, nc)
-    def _(k):
-        copy1(k).wait_send()
-
-    @pl.loop(1, nc * ns)
-    def _(k):
-        copy2(k, me).wait_send()
+        copy2(c_me, s_me, me, k).wait_send()
+
+
+def finish(updated, predictions, updated_out, predictions_out, done):
+    moves = [
+        pltpu.make_async_copy(updated, updated_out, done.at[0]),
+        pltpu.make_async_copy(predictions, predictions_out, done.at[1]),
+    ]
+    for move in moves:
+        move.start()
+    for move in moves:
+        move.wait()
 
 
 def shards(cell_points, magnetization, cell_level, suscept, inducing, stations):
@@ -213,6 +286,7 @@
     owned = block // ns
     targets = stations.shape[1]
     share = targets // nc
+    slots = nc if nc * share * block * 8 <= 1 << 24 else 1
     f32 = jnp.float32
     vmem = pl.BlockSpec(memory_space=pltpu.VMEM)
     hbm = pl.BlockSpec(memory_space=pltpu.HBM)
@@ -233,9 +307,11 @@
             pltpu.VMEM((nc, 8, block), f32),
             pltpu.VMEM((3, owned, LANES), f32),
             pltpu.VMEM((3, owned, LANES), f32),
-            pltpu.VMEM((nc * ns, 4, owned), f32),
+            pltpu.VMEM((nc * ns, 8, owned), f32),
             pltpu.VMEM((4, share, LANES), f32),
             pltpu.VMEM((share, LANES), f32),
+            pltpu.VMEM((2 * slots, share, block), f32),
+            pltpu.VMEM((3, block), f32),
             dma((nc,)),
             dma((nc,)),
             dma((nc * ns,)),
@@ -253,6 +329,14 @@
         inducing,
         stations,
     )
+    anywhere = pl.BlockSpec(memory_space=pl.ANY)
+    updated, predictions = pl.pallas_call(
+        finish,
+        out_shape=(jax.ShapeDtypeStruct((3, owned), f32), jax.ShapeDtypeStruct((1, share), f32)),
+        in_specs=[anywhere, anywhere],
+        out_specs=(anywhere, anywhere),
+        scratch_shapes=[dma((2,))],
+    )(updated, predictions)
     return updated, predictions.reshape(share)
 
 

time: 30.5 us -> 28.8 us (0.944)
  local copies, waits for them, and re-layouts: 1.82 us -> 0 us
    unnamed x6 -> x0, local copies, waits for them, and re-layouts: 1.82 us -> none
    pallas_call x0 -> x1, Pallas kernels: none -> 1.26 us  [shards(): pl.pallas_call(finish, out_shape=(jax.ShapeDtypeStruct((3, owned), f32),...]
    pallas_call x1, Pallas kernels: 27.8 us -> 26.7 us  [shards(): pl.pallas_call(functools.partial(kernel, nc, ns), out_shape=(jax.ShapeDty...]
where the time goes in v3:
time: 28.8 us; the launch traced here: 28.6 us
  Pallas kernels  28 us (97%)
  between operations  0.64 us (2%)
    pallas_call x1, Pallas kernels, shards(): pl.pallas_call(functools.partial(kernel, nc, ns), out_shape=(jax.ShapeDty...  26.7 us
    pallas_call x1, Pallas kernels, shards(): pl.pallas_call(finish, out_shape=(jax.ShapeDtypeStruct((3, owned), f32),...  1.26 us

profile of v3, /device:TPU:0, one launch (start us, length us, event | category | flops | bytes accessed | tf_op | source)
XLA Modules:
  0.0 28.6 jit_solution(14008955208116880766)
XLA Ops:
  0.6 26.7 %shard_map.77 = (f32[3,256]{1,0:T(4,128)}, f32[1,128]{1,0:T(1,128)}) custom-call(f32[3,1024]{1,0:T(4,128)} %cp_hbm.1, f32[3,1024]{1,0:T(4,128)} %mg_hbm.1, s32[1,1024]{1,0:T(1,128)} %bitcast.3, f32[1,1024]{1,0:T(1,128)} %bitcast.4, f32[3]{0:T(128)} %ind_hbm.1, f32[3,1024]{1,0:T(4,128)} %st_hbm.1), custom_call_target="tpu_custom_call" | custom-call | tf_op jit(solution)/shard_map/pallas_call | solution.py:294
  27.4 1.3 %shard_map.78 = (f32[3,256]{1,0:T(4,128)}, f32[1,128]{1,0:T(1,128)}) custom-call(f32[3,256]{1,0:T(4,128)} %get-tuple-element.6.updated, f32[1,128]{1,0:T(1,128)} %get-tuple-element.7.predictions), custom_call_target="tpu_custom_call" | custom-call | tf_op jit(solution)/shard_map/pallas_call | solution.py:333

commit v4 on v3

--- a/solution.py
+++ b/solution.py
@@ -164,21 +164,21 @@
     here = [cp[d : d + 1, own] for d in range(3)]
     mag[me, 4:5, :] = scaled[0] * here[0] + scaled[1] * here[1] + scaled[2] * here[2]
 
-    def copy2(c_who, s_who, slot, k):
+    def copy2(c_who, s_who, kc):
         return pltpu.make_async_remote_copy(
-            src_ref=mag.at[me], dst_ref=mag.at[slot], send_sem=send2.at[k], recv_sem=recv2.at[slot],
+            src_ref=mag.at[me], dst_ref=mag.at[me], send_sem=send2.at[0], recv_sem=recv2.at[kc],
             device_id={"cell": c_who, "stn": s_who}, device_id_type=MESH,
         )
 
     s_others = [partner(s_me, ks, ns) for ks in range(ns)]
     for ks in range(1, ns):
-        copy2(c_me, s_others[ks], me, ks).start()
+        copy2(c_me, s_others[ks], 0).start()
 
     @pl.loop(1, nc)
     def _(kc):
         c_who = partner(c_me, kc, nc)
         for ks in range(ns):
-            copy2(c_who, s_others[ks], me, kc * ns + ks).start()
+            copy2(c_who, s_others[ks], kc).start()
 
     for d in range(3):
         upd[d : d + 1, :] = new[d]
@@ -235,13 +235,11 @@
         def _(kc):
             geometry(kc, kc)
 
-    for t in range(ns):
-
-        @pl.when(s_me != t)
-        def _():
-            slot = c_me * ns + t
-            copy2(c_me, t, slot, 0).wait_recv()
-
+    def wait_pieces(sem, count):
+        held = mag.at[pl.ds(0, count)]
+        pltpu.make_async_copy(held, held, sem).wait()
+
+    wait_pieces(recv2.at[0], ns - 1)
     if slots == 1:
         geometry(0, 0)
     predict(c_me, 0)
@@ -249,8 +247,7 @@
     @pl.loop(1, nc)
     def _(kc):
         c_who = partner(c_me, kc, nc)
-        for t in range(ns):
-            copy2(c_who, t, c_who * ns + t, 0).wait_recv()
+        wait_pieces(recv2.at[kc], ns)
         if slots == 1:
             geometry(kc, 0)
             predict(c_who, 0)
@@ -263,9 +260,7 @@
     def _(k):
         copy1(k).wait_send()
 
-    @pl.loop(1, nc * ns)
-    def _(k):
-        copy2(c_me, s_me, me, k).wait_send()
+    wait_pieces(send2.at[0], nc * ns - 1)
 
 
 def finish(updated, predictions, updated_out, predictions_out, done):
@@ -314,8 +309,8 @@
             pltpu.VMEM((3, block), f32),
             dma((nc,)),
             dma((nc,)),
-            dma((nc * ns,)),
-            dma((nc * ns,)),
+            dma((1,)),
+            dma((nc,)),
             dma((6,)),
         ],
         compiler_params=pltpu.CompilerParams(

time: 28.8 us -> 28.1 us (0.976)
  Pallas kernels: 28 us -> 27.3 us
    pallas_call x1, Pallas kernels: 26.7 us -> 26 us  [shards(): pl.pallas_call(functools.partial(kernel, nc, ns), out_shape=(jax.ShapeDty...]
where the time goes in v4:
time: 28.1 us; the launch traced here: 27.9 us
  Pallas kernels  27.3 us (97%)
  between operations  0.64 us (2%)
    pallas_call x1, Pallas kernels, shards(): pl.pallas_call(functools.partial(kernel, nc, ns), out_shape=(jax.ShapeDty...  26 us
    pallas_call x1, Pallas kernels, shards(): pl.pallas_call(finish, out_shape=(jax.ShapeDtypeStruct((3, owned), f32),...  1.26 us

profile of v4, /device:TPU:0, one launch (start us, length us, event | category | flops | bytes accessed | tf_op | source)
XLA Modules:
  0.0 27.9 jit_solution(8036920562324629613)
XLA Ops:
  0.6 26.0 %shard_map.77 = (f32[3,256]{1,0:T(4,128)}, f32[1,128]{1,0:T(1,128)}) custom-call(f32[3,1024]{1,0:T(4,128)} %cp_hbm.1, f32[3,1024]{1,0:T(4,128)} %mg_hbm.1, s32[1,1024]{1,0:T(1,128)} %bitcast.3, f32[1,1024]{1,0:T(1,128)} %bitcast.4, f32[3]{0:T(128)} %ind_hbm.1, f32[3,1024]{1,0:T(4,128)} %st_hbm.1), custom_call_target="tpu_custom_call" | custom-call | tf_op jit(solution)/shard_map/pallas_call | solution.py:289
  26.7 1.3 %shard_map.78 = (f32[3,256]{1,0:T(4,128)}, f32[1,128]{1,0:T(1,128)}) custom-call(f32[3,256]{1,0:T(4,128)} %get-tuple-element.6.updated, f32[1,128]{1,0:T(1,128)} %get-tuple-element.7.predictions), custom_call_target="tpu_custom_call" | custom-call | tf_op jit(solution)/shard_map/pallas_call | solution.py:328

commit v5 on v4

--- a/solution.py
+++ b/solution.py
@@ -96,15 +96,6 @@
             tgt[d, t * LANES : (t + 1) * LANES, :] = jnp.broadcast_to(row, (LANES, LANES)).T
     acc[...] = jnp.zeros_like(acc)
 
-    for load in loads[4:]:
-        load.wait()
-    mine = pl.ds(pl.multiple_of(c_me * share, LANES), share)
-    place = [jnp.broadcast_to(st[d : d + 1, mine], (LANES, share)).T for d in range(3)]
-    for d in range(3):
-        stb[d] = place[d]
-    stb[3] = place[0] * ix + place[1] * iy + place[2] * iz
-    racc[...] = jnp.zeros_like(racc)
-
     def sweep(src):
         third[...] = src[3:6, :] * (1.0 / 3.0)
 
@@ -153,6 +144,8 @@
         copy1(k).wait_recv()
         sweep(gath.at[k])
 
+    for load in loads[4:]:
+        load.wait()
     gain = su[0:1, own]
     c_own = cvol[0:1, own]
     me = c_me * ns + s_me
@@ -182,6 +175,13 @@
 
     for d in range(3):
         upd[d : d + 1, :] = new[d]
+
+    mine = pl.ds(pl.multiple_of(c_me * share, LANES), share)
+    place = [jnp.broadcast_to(st[d : d + 1, mine], (LANES, share)).T for d in range(3)]
+    for d in range(3):
+        stb[d] = place[d]
+    stb[3] = place[0] * ix + place[1] * iy + place[2] * iz
+    racc[...] = jnp.zeros_like(racc)
 
     slots = geo.shape[0] // 2
     chunks_in = block // LANES

time: 28.1 us -> 28.1 us (level)
  no operation moved by 1% of the time
where the time goes in v5:
time: 28.1 us; the launch traced here: 27.9 us
  Pallas kernels  27.3 us (97%)
  between operations  0.64 us (2%)
    pallas_call x1, Pallas kernels, shards(): pl.pallas_call(functools.partial(kernel, nc, ns), out_shape=(jax.ShapeDty...  26 us
    pallas_call x1, Pallas kernels, shards(): pl.pallas_call(finish, out_shape=(jax.ShapeDtypeStruct((3, owned), f32),...  1.26 us

profile of v5, /device:TPU:0, one launch (start us, length us, event | category | flops | bytes accessed | tf_op | source)
XLA Modules:
  0.0 27.9 jit_solution(15430382832760989558)
XLA Ops:
  0.6 26.0 %shard_map.77 = (f32[3,256]{1,0:T(4,128)}, f32[1,128]{1,0:T(1,128)}) custom-call(f32[3,1024]{1,0:T(4,128)} %cp_hbm.1, f32[3,1024]{1,0:T(4,128)} %mg_hbm.1, s32[1,1024]{1,0:T(1,128)} %bitcast.3, f32[1,1024]{1,0:T(1,128)} %bitcast.4, f32[3]{0:T(128)} %ind_hbm.1, f32[3,1024]{1,0:T(4,128)} %st_hbm.1), custom_call_target="tpu_custom_call" | custom-call | tf_op jit(solution)/shard_map/pallas_call | solution.py:289
  26.7 1.3 %shard_map.78 = (f32[3,256]{1,0:T(4,128)}, f32[1,128]{1,0:T(1,128)}) custom-call(f32[3,256]{1,0:T(4,128)} %get-tuple-element.6.updated, f32[1,128]{1,0:T(1,128)} %get-tuple-element.7.predictions), custom_call_target="tpu_custom_call" | custom-call | tf_op jit(solution)/shard_map/pallas_call | solution.py:328
